TPU v7x, 32 devices: a whole 2x2x4 slice. The times are simulated.
32 devices in a mesh: gx: 8 (over y, x, core), wa: 4 (over z).
Axes of the slice: x: 2, y: 2, z: 4, core: 2. Of those that a mesh axis runs over, the one named last changes fastest.
Arguments:
- les_flow: bfloat16 [4, 512, 32, 256], P(None, 'gx', None, 'wa'), may hold values from -2.5 to 2.5
- y_index: int32 [128], replicated, may hold values from 0 to 254
- y_weight: bfloat16 [128], replicated, may hold values from 0 to 1
- acoustic_state: float32 [4, 1024, 64, 128], P(None, 'gx', 'wa'), may hold values from -6 to 6
Outputs:
- advanced_state: float32 [4, 1024, 64, 128], P(None, 'gx', 'wa')
All inputs are finite; a program needn't handle non-finite values.
Results may differ from a plain program's by a relative error of at most 0.0014.
Values may be sent and summed in bfloat16 or wider, within the bound.
No kernel may reach another device: no remote copies, remote signals or barrier semaphores. Data moves between devices by JAX's collectives and lax.ppermute only.
A program may use at most 128 MiB of HBM per device.

v0:
```python
import functools

import jax
import jax.numpy as jnp
from jax import lax
from jax.experimental import pallas as pl
from jax.experimental.pallas import tpu as pltpu
from jax.sharding import PartitionSpec as P

time_step = 0.4
unit = time_step / 12.0
reach = 8
ahead = 4
layers = 4
pad = 8
group = 3
f32 = jnp.float32
bf16 = jnp.bfloat16
grant = 60 * 2**20
vmem = pl.BlockSpec(memory_space=pltpu.VMEM)
hbm = pl.BlockSpec(memory_space=pl.ANY)


def shape_of(*dims, dtype=f32):
    return jax.ShapeDtypeStruct(dims, dtype)


def call(kernel, out_shape, in_specs, out_specs, scratch=()):
    return pl.pallas_call(
        kernel,
        out_shape=out_shape,
        in_specs=in_specs,
        out_specs=out_specs,
        scratch_shapes=list(scratch),
        compiler_params=pltpu.CompilerParams(vmem_limit_bytes=grant),
    )


def edge(axis):
    me = lax.axis_index(axis)
    return (me == 0, me == lax.axis_size(axis) - 1)


def up(value):
    return pltpu.roll(value, 1, 0)


def down(value):
    return pltpu.roll(value, 7, 0)


def side_by_side(les, pair, column):
    return jnp.concatenate(
        [les[2 * pair, column].astype(f32), les[2 * pair + 1, column].astype(f32)], axis=1
    )


def cut_kernel(les, state, *refs):
    *tiles, first, last, wide, ends, sem = refs
    devices = len(tiles)
    columns, levels, width = les.shape[1:]
    own = levels // devices
    me = lax.axis_index("wa")
    starts = (0, state.shape[1] - reach)
    copies = [
        pltpu.make_async_copy(state.at[:, pl.ds(starts[end], reach)], ends.at[end], sem.at[end])
        for end in range(2)
    ]
    for copy in copies:
        copy.start()

    def body(column, carry):
        for pair in range(2):
            wide[pair, column] = jnp.concatenate(
                [les[2 * pair, column].astype(f32), les[2 * pair + 1, column].astype(f32)], axis=1
            )
        return carry

    lax.fori_loop(0, columns, body, 0, unroll=8)
    for shift in range(devices):
        row = pl.multiple_of(lax.rem(me + shift, devices) * own, own)
        tiles[shift][...] = (
            wide[:, :, pl.ds(row, own), :].reshape(2 * columns * own, 2 * width).astype(bf16)
        )
    rows = 4 * reach * state.shape[2]
    les_rows = 2 * ahead * levels
    for end, (target, start) in enumerate(((first, 0), (last, columns - ahead))):
        copies[end].wait()
        target[pl.ds(0, rows), :] = ends[end].reshape(rows, 128).astype(bf16)
        target[pl.ds(rows, les_rows), :] = (
            wide[:, start : start + ahead].reshape(les_rows, 128).astype(bf16)
        )


def cut_tiles(les_flow, state, devices):
    _, columns, levels, width = les_flow.shape
    tile = shape_of(2 * columns * (levels // devices), 2 * width, dtype=bf16)
    end = shape_of(4 * reach * state.shape[2] + 2 * ahead * levels, 128, dtype=bf16)
    *tiles, first, last = call(
        cut_kernel,
        [tile] * devices + [end] * 2,
        [vmem, hbm],
        [vmem] * (devices + 2),
        [
            pltpu.VMEM((2, columns, levels, 2 * width), f32),
            pltpu.VMEM((2, 4, reach, state.shape[2], 128), f32),
            pltpu.SemaphoreType.DMA((2,)),
        ],
    )(les_flow, state)
    return (tiles, first, last)


def tails_kernel(skip, levels, before, after, *refs):
    tails, wide = (refs[:-1], refs[-1])
    devices = len(tails)
    own = levels // devices
    rows = 2 * ahead * levels
    wide[0] = before[pl.ds(skip, rows), :].astype(f32).reshape(2, ahead, levels, 128)
    wide[1] = after[pl.ds(skip, rows), :].astype(f32).reshape(2, ahead, levels, 128)
    me = lax.axis_index("wa")
    for shift in range(devices):
        row = pl.multiple_of(lax.rem(me + shift, devices) * own, own)
        tails[shift][...] = (
            wide[:, :, :, pl.ds(row, own), :].reshape(4 * ahead * own, 128).astype(bf16)
        )


def cut_tails(before, after, skip, levels, devices):
    tail = shape_of(4 * ahead * (levels // devices), 128, dtype=bf16)
    return call(
        functools.partial(tails_kernel, skip, levels),
        [tail] * devices,
        [vmem, vmem],
        [vmem] * devices,
        [pltpu.VMEM((2, 2, ahead, levels, 128), f32)],
    )(before, after)


def run_rows(s, run, height):
    first = max(0, reach - run * s)
    count = min(run, 8 * run - reach - run * s) - first
    inner = pl.ds(first * height, count * height)
    return (inner, pl.ds((run * s + first - reach) * height, count * height))


def widen_kernel(state, before, after, out, send_low, send_high, whole, result, sem, out_sem):
    height, run = out.shape[1:3]
    pitch = run * height + pad
    flat_whole = whole.reshape(32 * pitch, 128)
    fetches = []
    for f in range(4):
        for s in range(8):
            inner, outer = run_rows(s, run, height)
            fetches.append(
                pltpu.make_async_copy(state.at[f, outer], whole.at[f, s, inner], sem.at[f, s])
            )
    for fetch in fetches:
        fetch.start()
    rows = reach * height
    for f in range(4):
        part = pl.ds(f * rows, rows)
        whole[f, 0, pl.ds(0, rows), :] = before[part, :].astype(f32)
        whole[f, 7, pl.ds(run * height - rows, rows), :] = after[part, :].astype(f32)
    pushes = []
    for f in range(4):
        for s in range(8):
            fetches[8 * f + s].wait()

        def body(step, carry, f=f):
            for p in range(4):
                for i in range(run):
                    start = f * 8 * pitch + i * height + 4 * step + p
                    result[f, 4 * step + p, i] = flat_whole[pl.ds(start, 8, stride=pitch), :]
            return carry

        lax.fori_loop(0, height // 4, body, 0)
        push = pltpu.make_async_copy(result.at[f], out.at[f], out_sem.at[f])
        push.start()
        pushes.append(push)
    cast_layers(result, send_low, send_high)
    for push in pushes:
        push.wait()


def cast_layers(result, send_low, send_high):
    _, height, run = result.shape[:3]
    rows = run * 8
    for f in range(4):
        for z in range(layers):
            at = pl.ds((f * layers + z) * rows, rows)
            send_low[at, :] = result[f, z].reshape(rows, 128).astype(bf16)
            send_high[at, :] = result[f, height - layers + z].reshape(rows, 128).astype(bf16)


def widen(state, before, after):
    columns, height = state.shape[1:3]
    run = (columns + 2 * reach) // 8
    layer = shape_of(4 * layers * run * 8, 128, dtype=bf16)
    return call(
        widen_kernel,
        [shape_of(4, height, run, 8, 128), layer, layer],
        [hbm, vmem, vmem],
        [hbm, vmem, vmem],
        [
            pltpu.VMEM((4, 8, run * height + pad, 128), f32),
            pltpu.VMEM((4, height, run, 8, 128), f32),
            pltpu.SemaphoreType.DMA((4, 8)),
            pltpu.SemaphoreType.DMA((4,)),
        ],
    )(state.reshape(4, columns * height, 128), before, after)


def spread_kernel(devices, width, *refs):
    tiles, tails = (refs[:devices], refs[devices : 2 * devices])
    y_index, y_weight, out, send_low, send_high, wide = refs[2 * devices :]
    me = lax.axis_index("wa")
    left_weight = (1.0 - y_weight[...].astype(f32)).astype(bf16).astype(f32)
    right_weight = y_weight[...].astype(f32)
    row_ids = lax.broadcasted_iota(jnp.int32, (width, 128), 0)
    nothing = jnp.zeros((width, 128), f32)
    total, tail = (None, None)
    for shift in range(devices):
        first_row = lax.rem(me - shift + devices, devices) * width
        gap = y_index[...] - first_row - row_ids
        matrix = jnp.where(gap == 0, left_weight, 0.0) + jnp.where(gap == -1, right_weight, 0.0)
        pair = jnp.concatenate(
            [
                jnp.concatenate([matrix, nothing], axis=1),
                jnp.concatenate([nothing, matrix], axis=1),
            ],
            axis=0,
        ).astype(bf16)
        part = jnp.dot(tiles[shift][...], pair, preferred_element_type=f32)
        tail_part = jnp.dot(tails[shift][...], pair, preferred_element_type=f32)
        total = part if total is None else total + part
        tail = tail_part if tail is None else tail + tail_part
    levels, run = (out.shape[1], out.shape[2] - 1)
    columns = total.shape[0] // (2 * levels)
    wide_columns = columns + 2 * ahead
    _, is_end = edge("gx")
    for f in range(4):
        pair, lanes = (f // 2, slice(128 * (f % 2), 128 * (f % 2 + 1)))
        main = total[pair * columns * levels : (pair + 1) * columns * levels, lanes]
        side = ahead * levels
        left = tail[pair * side : (pair + 1) * side, lanes]
        right = tail[(2 + pair) * side : (3 + pair) * side, lanes]
        right = jnp.where(is_end, jnp.concatenate([main[-levels:]] * ahead, axis=0), right)
        wide[pl.ds(f * wide_columns * levels, wide_columns * levels), :] = jnp.concatenate(
            [left, main, right], axis=0
        )
    for f in range(4):

        def body(k, carry, f=f):
            for j in range(run):
                start = (f * wide_columns + j) * levels + k
                value = wide[pl.ds(start, 8, stride=run * levels), :]
                out[f, k, j] = value
                if j == 0:
                    out[f, k, run] = down(value)
            return carry

        lax.fori_loop(0, levels, body, 0)
        rows = run * 8
        at = pl.ds(f * rows, rows)
        send_high[at, :] = out[f, levels - 1, :run].reshape(rows, 128).astype(bf16)
        for k in range(2):
            send_low[k, at, :] = out[f, k, :run].reshape(rows, 128).astype(bf16)


def spread(tiles, tails, y_index, y_weight, columns, levels, width):
    devices = len(tiles)
    run = (columns + 2 * ahead) // 8
    return call(
        functools.partial(spread_kernel, devices, width),
        [
            shape_of(4, levels, run + 1, 8, 128),
            shape_of(2, 4 * run * 8, 128, dtype=bf16),
            shape_of(4 * run * 8, 128, dtype=bf16),
        ],
        [vmem] * (2 * devices + 2),
        [vmem] * 3,
        [pltpu.VMEM((4 * (columns + 2 * ahead) * levels, 128), f32)],
    )(*tiles, *tails, y_index.reshape(1, 128), y_weight.reshape(1, 128))


def band_matrix():
    row, column = [lax.broadcasted_iota(jnp.int32, (256, 256), axis) for axis in range(2)]
    gap = jnp.where((row < 128) == (column < 128), row - column, 128)
    near = jnp.where(gap == 1, 8.0, jnp.where(gap == -1, -8.0, 0.0))
    return (near + jnp.where(gap == 2, -1.0, jnp.where(gap == -2, 1.0, 0.0))).astype(bf16)


def difference(low_far, low, high, high_far):
    return 8.0 * (high - low) - (high_far - low_far)


def spanwise(source, plane, slopes, band):
    run = source.shape[2] - 4
    for pair in range(2):
        sides = [
            source[f, pl.ds(plane, 2), pl.ds(2, run)].reshape(2 * run * 8, 128).astype(bf16)
            for f in (2 * pair, 2 * pair + 1)
        ]
        both = jnp.dot(jnp.concatenate(sides, axis=1), band, preferred_element_type=f32)
        slopes[2 * pair] = both[:, :128].reshape(2, run, 8, 128)
        slopes[2 * pair + 1] = both[:, 128:].reshape(2, run, 8, 128)


def stage(source, plane, coeffs, across, anchor, store, slopes_y, factor):
    run = coeffs.shape[2]
    places = [(p, u) for p in range(2) for u in range(group)]
    for first in range(0, run, group):
        speeds = {
            (f, p, u): coeffs[f, across + p, first + u] for f in range(3) for p, u in places
        }
        rates, spreads, own_rates, centers = ({}, {}, {}, {})
        for f in range(4):
            line = {
                (p, u): source[f, plane + p, first + u + 2]
                for p in range(2)
                for u in range(-2, group + 2)
            }
            for u in range(group):
                for p in (-2, -1, 2, 3):
                    line[p, u] = source[f, plane + p, first + u + 2]
            for p, u in places:
                slope_x = difference(*[line[p, u + k] for k in (-2, -1, 1, 2)])
                slope_z = difference(*[line[p + k, u] for k in (-2, -1, 1, 2)])
                slope_y = slopes_y[f, p, first + u]
                rate = (
                    speeds[0, p, u] * slope_x + speeds[1, p, u] * slope_y + speeds[2, p, u] * slope_z
                )
                if f == 0:
                    own_rates[p, u] = rate
                    centers[p, u] = line[p, u]
                    for k, slope in enumerate((slope_x, slope_y, slope_z)):
                        rates[k + 1, p, u] = unit * slope
                else:
                    rate += rates[f, p, u]
                    start = line[p, u] if anchor is None else anchor(f, p, first + u)
                    store(f, p, first + u, start - factor * rate)
                    slope = (slope_x, slope_y, slope_z)[f - 1]
                    spreads[p, u] = slope if f == 1 else spreads[p, u] + slope
        for p, u in places:
            rate = own_rates[p, u] + coeffs[3, across + p, first + u] * spreads[p, u]
            start = centers[p, u] if anchor is None else anchor(0, p, first + u)
            store(0, p, first + u, start - factor * rate)


def fill_coeffs(flow, level, coeffs, plane):
    run = coeffs.shape[2]
    for f in range(4):
        here = [flow[f, level, j] for j in range(run // 2 + 1)]
        above = [flow[f, level + 1, j] for j in range(run // 2 + 1)]
        middle = [0.5 * (a + b) for a, b in zip(here, above)]
        for p, line in enumerate((here, middle)):
            for i in range(run):
                j = i // 2
                value = line[j] if i % 2 == 0 else 0.5 * (line[j] + line[j + 1])
                if f < 3:
                    value = (0.3 * unit) * value
                else:
                    speed = 1.0 + 0.2 * value
                    value = unit * (speed * speed)
                coeffs[f, plane + p, i] = value


def put_plane(target, f, plane, values):
    run = len(values)
    for i, value in enumerate(values):
        target[f, plane, i + 2] = value
    for i in range(2):
        target[f, plane, i] = up(values[run - 2 + i])
        target[f, plane, run + 2 + i] = down(values[i])


def close_planes(target, plane):
    run = target.shape[2] - 4
    for f in range(4):
        for i in range(2):
            target[f, plane, i] = up(target[f, plane, run + i])
            target[f, plane, run + 2 + i] = down(target[f, plane, 2 + i])


def mask_columns(target, planes, offset, left, right):
    run = target.shape[2] - 2 * offset
    sublane = lax.broadcasted_iota(jnp.int32, (8, 128), 0)

    @pl.when(left)
    def _():
        for f in range(4):
            for plane in planes:
                for i in range(reach):
                    value = target[f, plane, offset + i]
                    target[f, plane, offset + i] = jnp.where(sublane == 0, 0.0, value)

    @pl.when(right)
    def _():
        for f in range(4):
            for plane in planes:
                for i in range(run - reach, run):
                    value = target[f, plane, offset + i]
                    target[f, plane, offset + i] = jnp.where(sublane == 7, 0.0, value)


class Sweep:
    def __init__(self, fields, middle, coeffs, slopes, flow, result, base, factors, shift):
        self.fields, self.middle, self.coeffs, self.slopes = (fields, middle, coeffs, slopes)
        self.flow, self.result, self.base, self.factors = (flow, result, base, factors)
        self.shift = shift
        self.run = coeffs.shape[2]
        self.band = band_matrix()
        self.left, self.right = edge("gx")

    def fill(self, step):
        fill_coeffs(self.flow, step, self.coeffs, 2 * step)

    def first_slopes(self, step, slot=0):
        spanwise(self.fields, 2 * step + 2, self.slopes.at[slot], self.band)

    def first(self, step, slot=0):
        run, middle, base = (self.run, self.middle, self.base)

        def store(f, p, i, value):
            plane = 2 * step + p
            middle[f, plane, i + 2] = value
            if i < 2:
                middle[f, plane, run + 2 + i] = down(value)
            if i >= run - 2:
                middle[f, plane, i - (run - 2)] = up(value)

        anchor = None
        if base is not None:

            def anchor(f, p, i):
                return base[f, 2 * step + p, i]

        stage(
            self.fields, 2 * step + 2, self.coeffs, 2 * step, anchor, store,
            self.slopes.at[slot], self.factors[0],
        )

    def mask_first(self, step):
        mask_columns(self.middle, [2 * step, 2 * step + 1], 2, self.left, self.right)

    def clear_first(self, step):
        for f in range(4):
            for p in range(2):
                for i in range(self.run + 4):
                    self.middle[f, 2 * step + p, i] = jnp.zeros((8, 128), f32)

    def last_slopes(self, step, slot=2):
        spanwise(self.middle, 2 * step + 2, self.slopes.at[slot], self.band)

    def last(self, step, slot=2):
        run, result = (self.run, self.result)

        def anchor(f, p, i):
            if self.base is not None:
                return self.base[f, 2 * step + 2 + p, i]
            return self.fields[f, 2 * step + 4 + p, i + 2]

        def store(f, p, i, value):
            z = 2 * step + p
            if self.base is None:
                result[f, z - self.shift(step), i] = value
            else:
                pitch = result.shape[2]
                height = (pitch - pad) // run
                flat_result = result.reshape(32 * pitch, 128)
                flat_result[pl.ds(f * 8 * pitch + i * height + z, 8, stride=pitch), :] = value

        stage(
            self.middle, 2 * step + 2, self.coeffs, 2 * step + 2, anchor, store,
            self.slopes.at[slot], self.factors[1],
        )

    def mask_last(self, step):
        if self.base is None:
            first = 2 * step - self.shift(step)
            mask_columns(self.result, [first, first + 1], 0, self.left, self.right)


def inner_kernel(factors, final, *refs):
    if final:
        inner, outer, flow_in, anchor, out, edges = refs[:6]
        scratch = refs[6:]
        base, q_sem = scratch[-2:]
    else:
        state, flow_in, out, edges = refs[:4]
        scratch = refs[4:]
        base = None
    fields, middle, coeffs, result, slopes, flow, in_sem, out_sem, flow_sem = scratch[:9]
    run = coeffs.shape[2]
    levels = flow_in.shape[1]
    pairs = in_sem.shape[0]

    def source(pair):
        if not final:
            return state.at[:, pl.ds(2 * pair, 2)]
        if pair < 2:
            return outer.at[:, pl.ds(2 * pair, 2)]
        if pair >= pairs - 2:
            return outer.at[:, pl.ds(2 * (pair - (pairs - 4)), 2)]
        return inner.at[:, pl.ds(2 * (pair - 2), 2)]

    flow_copy = pltpu.make_async_copy(flow_in, flow.at[:, pl.ds(1, levels)], flow_sem)
    flow_copy.start()
    copies = []
    for pair in range(pairs):
        copies.append(
            [
                pltpu.make_async_copy(
                    source(pair),
                    fields.at[:, pl.ds(4 + 2 * pair, 2), pl.ds(2, run)],
                    in_sem.at[pair],
                )
            ]
        )
        if final:
            copies[-1].append(
                pltpu.make_async_copy(
                    anchor.at[:, pl.ds(2 * pair, 2)],
                    base.at[:, pl.ds(2 + 2 * pair, 2)],
                    q_sem.at[pair],
                )
            )
        for copy in copies[-1]:
            copy.start()
    sweep = Sweep(
        fields, middle, coeffs, slopes, flow, result, base, factors, lambda step: layers
    )

    def prepare(pair):
        for copy in copies[pair]:
            copy.wait()
        for p in range(2):
            close_planes(fields, 4 + 2 * pair + p)

    flow_copy.wait()
    for pair in range(4):
        prepare(pair)

    def begin(step, carry):
        sweep.fill(step)
        sweep.first_slopes(step)
        sweep.first(step)
        sweep.mask_first(step)
        return carry

    lax.fori_loop(2, 4, begin, 0)
    for pair in range(4, pairs):
        prepare(pair)
    begin(4, 0)

    def body(step, carry):
        sweep.fill(step + 3)
        sweep.last_slopes(step)
        sweep.first_slopes(step + 3)
        sweep.last(step)
        sweep.first(step + 3)
        sweep.mask_last(step)
        sweep.mask_first(step + 3)
        return carry

    lax.fori_loop(2, pairs - 3, body, 0)
    pushes = [
        pltpu.make_async_copy(
            middle.at[:, pl.ds(4 + 8 * end, 4)], edges.at[:, pl.ds(4 * end, 4)], out_sem.at[end]
        )
        for end in range(2)
    ]
    for push in pushes:
        push.start()
    sweep.last_slopes(pairs - 3)
    sweep.last(pairs - 3)
    sweep.mask_last(pairs - 3)
    pushes.append(pltpu.make_async_copy(result, out, out_sem.at[2]))
    pushes[-1].start()
    for push in pushes:
        push.wait()


def outer_kernel(factors, final, *refs):
    state, edges, low, high, flow_in, below, above = refs[:7]
    if final:
        anchor, q_low, q_high, part, out = refs[7:12]
        scratch = refs[12:]
        base, q_sem, part_sem = scratch[-3:]
    else:
        out, send_low, send_high = refs[7:10]
        scratch = refs[10:]
        base = None
    fields, middle, coeffs, result, slopes, flow, in_sem, out_sem, flow_sem = scratch[:9]
    run = coeffs.shape[2]
    levels = flow_in.shape[1]
    height = fields.shape[1] - 2 * layers
    rows = run * 8
    lower, upper = edge("wa")
    flow_copy = pltpu.make_async_copy(flow_in, flow.at[:, pl.ds(1, levels)], flow_sem)
    flow_copy.start()
    far = state.shape[1] - 4

    def fetch(half):
        copies = [
            pltpu.make_async_copy(
                state.at[:, pl.ds(far * half, 4)],
                fields.at[:, pl.ds(4 + 12 * half, 4), pl.ds(2, run)],
                in_sem.at[half],
            ),
            pltpu.make_async_copy(
                edges.at[:, pl.ds(4 * half, 4)],
                middle.at[:, pl.ds(4 + 8 * half, 4)],
                in_sem.at[2 + half],
            ),
        ]
        if final:
            copies.append(
                pltpu.make_async_copy(
                    anchor.at[:, pl.ds(12 * half, 4)],
                    base.at[:, pl.ds(2 + 12 * half, 4)],
                    q_sem.at[half],
                )
            )
        return copies

    for half in range(2):
        for copy in fetch(half):
            copy.start()
    if final:
        part_copy = pltpu.make_async_copy(part, result, part_sem)
        part_copy.start()

    def layer(ref, f, z):
        value = ref[pl.ds((f * layers + z) * rows, rows), :].astype(f32)
        return [value[8 * i : 8 * i + 8] for i in range(run)]

    for f in range(4):
        for z in range(layers):
            put_plane(fields, f, z, layer(low, f, z))
            put_plane(fields, f, layers + height + z, layer(high, f, z))
        if final:
            for z in range(2):
                for target, ref, from_z in ((z, q_low, layers - 2 + z), (height + 2 + z, q_high, z)):
                    for i, value in enumerate(layer(ref, f, from_z)):
                        base[f, target, i] = value
    flow_copy.wait()
    half_run = run // 2
    for f in range(4):
        at = pl.ds(f * half_run * 8, half_run * 8)
        under, over, over_next = (below[at, :], above[0, at, :], above[1, at, :])
        for j in range(half_run):
            piece = slice(8 * j, 8 * j + 8)
            values = (
                under[piece].astype(f32),
                jnp.where(upper, flow[f, levels, j], over[piece].astype(f32)),
                over_next[piece].astype(f32),
            )
            for level, value in zip((0, levels + 1, levels + 2), values):
                flow[f, level, j] = value
                if j == 0:
                    flow[f, level, half_run] = down(value)
    if final:
        part_copy.wait()
    sweep = Sweep(
        fields, middle, coeffs, slopes, flow, result, base, factors, lambda step: 8 * (step // 4)
    )

    def push(half):
        planes = pl.ds(4 * half, 4)
        return pltpu.make_async_copy(result.at[:, planes], out.at[:, planes], out_sem.at[half])

    def body(half, carry):
        for copy in fetch(half):
            copy.wait()
        for p in range(4):
            close_planes(fields, 4 + 12 * half + p)
        for k in range(2):
            sweep.first_slopes(8 * half + k, k)
        for k in range(3):
            sweep.fill(7 * half + k)
        for k in range(2):
            sweep.first(8 * half + k, k)
        for k in range(2):
            sweep.mask_first(8 * half + k)

        @pl.when(lower & (half == 0))
        def _():
            sweep.clear_first(0)

        @pl.when(upper & (half == 1))
        def _():
            sweep.clear_first(9)

        for k in range(2):
            sweep.last_slopes(6 * half + k, 2 + k)
        for k in range(2):
            sweep.last(6 * half + k, 2 + k)
        for k in range(2):
            sweep.mask_last(6 * half + k)
        if not final:
            push(half).start()
        return carry

    lax.fori_loop(0, 2, body, 0)
    if final:
        pushes = []
        for s in range(8):
            inner, outer = run_rows(s, run, height)
            pushes.append(
                pltpu.make_async_copy(result.at[:, s, inner], out.at[:, outer], out_sem.at[s])
            )
        for copy in pushes:
            copy.start()
        for copy in pushes:
            copy.wait()
    else:
        cast_layers(result, send_low, send_high)
        for half in range(2):
            push(half).wait()


def advance(height, run, halo, flow, factors, state=None, parts=None, anchor=None, anchor_halo=None):
    final = anchor is not None
    flow, below, above = flow
    pairs = height // 2
    natural = (4, 8, run * height + pad, 128)
    half_block = (4, height // 2, run, 8, 128)
    inner_result = natural if final else half_block
    common = [
        pltpu.VMEM((4, height + 2 * layers, run + 4, 8, 128), f32),
        pltpu.VMEM((4, height + 4, run + 4, 8, 128), f32),
        pltpu.VMEM((4, height + 4, run, 8, 128), f32),
        pltpu.VMEM(inner_result, f32),
        pltpu.VMEM((4, 4, 2, run, 8, 128), f32),
        pltpu.VMEM((4, flow.shape[1] + 3, run // 2 + 1, 8, 128), f32),
    ]
    sems = [
        pltpu.SemaphoreType.DMA((pairs,)),
        pltpu.SemaphoreType.DMA((8,)),
        pltpu.SemaphoreType.DMA,
    ]
    base = pltpu.VMEM((4, height + 4, run, 8, 128), f32)
    edges_shape = shape_of(4, 8, run + 4, 8, 128)
    operands = [*parts, flow, anchor] if final else [state, flow]
    inner, edges = call(
        functools.partial(inner_kernel, factors, final),
        [shape_of(*inner_result), edges_shape],
        [hbm] * len(operands),
        [hbm, hbm],
        common + sems + ([base, pltpu.SemaphoreType.DMA((pairs,))] if final else []),
    )(*operands)
    operands = [parts[1] if final else state, edges, *halo, flow, below, above]
    in_specs = [hbm, hbm, vmem, vmem, hbm, vmem, vmem]
    if final:
        (out,) = call(
            functools.partial(outer_kernel, factors, final),
            [shape_of(4, (run * 8 - 2 * reach) * height, 128)],
            in_specs + [hbm, vmem, vmem, hbm],
            [hbm],
            common + sems + [base, pltpu.SemaphoreType.DMA((2,)), pltpu.SemaphoreType.DMA],
        )(*operands, anchor, *anchor_halo, inner)
        return out
    layer = shape_of(4 * layers * run * 8, 128, dtype=bf16)
    outer, send_low, send_high = call(
        functools.partial(outer_kernel, factors, final),
        [shape_of(*half_block), layer, layer],
        in_specs,
        [hbm, vmem, vmem],
        common + sems,
    )(*operands)
    return ((inner, outer), send_low, send_high)


def neighbours(axis, forward):
    count = lax.axis_size(axis)
    return [(i, i + 1) if forward else (i + 1, i) for i in range(count - 1)]


def exchange(to_next, to_previous, axis):
    return (
        lax.ppermute(to_next, axis, neighbours(axis, True)),
        lax.ppermute(to_previous, axis, neighbours(axis, False)),
    )


def to_owners(pieces):
    devices = len(pieces)
    moved = [pieces[0]]
    for shift in range(1, devices):
        ring = [(i, (i + shift) % devices) for i in range(devices)]
        moved.append(lax.ppermute(pieces[shift], "wa", ring))
    return moved


def shards(les_flow, y_index, y_weight, acoustic_state):
    devices = lax.axis_size("wa")
    _, columns, levels, width = les_flow.shape
    cut, first, last = cut_tiles(les_flow, acoustic_state, devices)
    tiles = to_owners(cut)
    before, after = exchange(last, first, "gx")
    skip = 4 * reach * acoustic_state.shape[2]
    tails = cut_tails(before, after, skip, levels, devices)
    before, after, *tails = lax.optimization_barrier((before, after, *tails))
    state, send_low, send_high = widen(acoustic_state, before, after)
    send_low, send_high, *late = lax.optimization_barrier((send_low, send_high, *tails[3:]))
    tails = to_owners(tails[:3] + late)
    tiles, tails, send_low, send_high = lax.optimization_barrier(
        (tiles, tails, send_low, send_high)
    )
    halo = exchange(send_high, send_low, "wa")
    flow, low, high = spread(
        tiles, tails, y_index, y_weight, columns, levels // devices, width
    )
    below, above = exchange(high, low, "wa")
    flow = (flow, below, above)
    height, run = state.shape[1:3]
    parts, send_low, send_high = advance(height, run, halo, flow, (1 / 4, 1 / 3), state=state)
    half_halo = exchange(send_high, send_low, "wa")
    result = advance(
        height, run, half_halo, flow, (1 / 2, 1.0), parts=parts, anchor=state, anchor_halo=halo
    )
    return result.reshape(acoustic_state.shape)


def solution(mesh):
    placed = (P(None, "gx", None, "wa"), P(), P(), P(None, "gx", "wa", None))
    return jax.shard_map(
        shards, mesh=mesh, in_specs=placed, out_specs=P(None, "gx", "wa", None), check_vma=False
    )
```

profile of v0, /device:TPU:0, one launch (start us, length us, event | category | flops | bytes accessed | tf_op | source)
XLA Modules:
  0.0 107.6 jit_solution(6878884128367918633)
XLA Ops:
  0.0 3.8 %shard_map.46 = (bf16[1024,128]{1,0:T(8,128)(2,1)}, bf16[1024,128]{1,0:T(8,128)(2,1)}, bf16[1024,128]{1,0:T(8,128)(2,1)}, bf16[1024,128]{1,0:T(8,128)(2,1)}, bf1...) custom-call(bf16[4,64,32,64]{3,2,1,0:T(8,128)(2,1)} %les.1, f32[4,128,16,128]{3,2,1,0:T(8,128)} %state.1), custom_call_target="tpu_custom_call" | custom-call | tf_op jit(solution)/shard_map/pallas_call | solution.py:99
  3.9 2.4 %collective-permute-start = (bf16[768,128]{1,0:T(8,128)(2,1)}, bf16[768,128]{1,0:T(8,128)(2,1)S(1)}, u32[]{:S(2)}, u32[]{:S(2)}) collective-permute-start(bf16[768,128]{1,0:T(8,128)(2,1)} %get-tuple-element.47), channel_id=1, source_target_pairs={{0,4},{4,8},{8,12},{12,16},{16,20},{20,24},{24,28},{1,5},{5,9},{9,... | collective-permute-start | bytes 589832 | tf_op jit(solution)/shard_map/ppermute | solution.py:782
  6.2 1.3 %collective-permute-start.1 = (bf16[768,128]{1,0:T(8,128)(2,1)}, bf16[768,128]{1,0:T(8,128)(2,1)S(1)}, u32[]{:S(2)}, u32[]{:S(2)}) collective-permute-start(bf16[768,128]{1,0:T(8,128)(2,1)} %get-tuple-element.48), channel_id=1, source_target_pairs={{4,0},{8,4},{12,8},{16,12},{20,16},{24,20},{28,24},{5,1},{9,5},{13... | collective-permute-start | bytes 589832 | tf_op jit(solution)/shard_map/ppermute | solution.py:783
  7.5 2.5 %collective-permute-start.2 = (bf16[1024,128]{1,0:T(8,128)(2,1)}, bf16[1024,128]{1,0:T(8,128)(2,1)S(1)}, u32[]{:S(2)}, u32[]{:S(2)}) collective-permute-start(bf16[1024,128]{1,0:T(8,128)(2,1)} %get-tuple-element.57), channel_id=1, source_target_pairs={{0,1},{1,2},{2,3},{3,0},{4,5},{5,6},{6,7},{7,4},{8,9},{9,10},{10,1... | collective-permute-start | bytes 786440 | tf_op jit(solution)/shard_map/ppermute | solution.py:792
  10.0 2.6 %collective-permute-start.3 = (bf16[1024,128]{1,0:T(8,128)(2,1)}, bf16[1024,128]{1,0:T(8,128)(2,1)S(1)}, u32[]{:S(2)}, u32[]{:S(2)}) collective-permute-start(bf16[1024,128]{1,0:T(8,128)(2,1)} %get-tuple-element.58), channel_id=1, source_target_pairs={{0,2},{1,3},{2,0},{3,1},{4,6},{5,7},{6,4},{7,5},{8,10},{9,11},{10,... | collective-permute-start | bytes 786440 | tf_op jit(solution)/shard_map/ppermute | solution.py:792
  12.6 1.3 %collective-permute-start.4 = (bf16[1024,128]{1,0:T(8,128)(2,1)}, bf16[1024,128]{1,0:T(8,128)(2,1)S(1)}, u32[]{:S(2)}, u32[]{:S(2)}) collective-permute-start(bf16[1024,128]{1,0:T(8,128)(2,1)} %get-tuple-element.59), channel_id=1, source_target_pairs={{0,3},{1,0},{2,1},{3,2},{4,7},{5,4},{6,5},{7,6},{8,11},{9,8},{10,9... | collective-permute-start | bytes 786440 | tf_op jit(solution)/shard_map/ppermute | solution.py:792
  15.3 1.7 %shard_map.47 = (bf16[128,128]{1,0:T(8,128)(2,1)}, bf16[128,128]{1,0:T(8,128)(2,1)}, bf16[128,128]{1,0:T(8,128)(2,1)}, bf16[128,128]{1,0:T(8,128)(2,1)}) custom-call(bf16[768,128]{1,0:T(8,128)(2,1)} %copy-done.2, bf16[768,128]{1,0:T(8,128)(2,1)} %copy-done.3), custom_call_target="tpu_custom_call" | custom-call | tf_op jit(solution)/shard_map/pallas_call | solution.py:130
  17.7 0.7 collective-permute-start.6
  18.4 6.0 %shard_map.48 = (f32[4,16,18,8,128]{4,3,2,1,0:T(8,128)}, bf16[2304,128]{1,0:T(8,128)(2,1)}, bf16[2304,128]{1,0:T(8,128)(2,1)}) custom-call(f32[4,2048,128]{2,1,0:T(8,128)} %bitcast.4, bf16[768,128]{1,0:T(8,128)(2,1)} %copy-done.2, bf16[768,128]{1,0:T(8,128)(2,1)} %copy-done.3), custom_call_target="tpu_custom_call" | custom-call | tf_op jit(solution)/shard_map/pallas_call | solution.py:199
  24.5 5.1 %collective-permute-done.5.refs_5_ = bf16[128,128]{1,0:T(8,128)(2,1)S(1)} collective-permute-done((bf16[128,128]{1,0:T(8,128)(2,1)}, bf16[128,128]{1,0:T(8,128)(2,1)S(1)}, u32[]{:S(2)}, u32[]{:S(2)}) %collective-permute-start.5) | collective-permute-done | bytes 32800 | tf_op jit(solution)/shard_map/ppermute | solution.py:792
  29.6 8.7 %collective-permute-done.6.refs_6_ = bf16[128,128]{1,0:T(8,128)(2,1)S(1)} collective-permute-done((bf16[128,128]{1,0:T(8,128)(2,1)}, bf16[128,128]{1,0:T(8,128)(2,1)S(1)}, u32[]{:S(2)}, u32[]{:S(2)}) %collective-permute-start.6) | collective-permute-done | bytes 32800 | tf_op jit(solution)/shard_map/ppermute | solution.py:792
  38.7 3.6 %collective-permute-start.8 = (bf16[2304,128]{1,0:T(8,128)(2,1)}, bf16[2304,128]{1,0:T(8,128)(2,1)S(1)}, u32[]{:S(2)}, u32[]{:S(2)}) collective-permute-start(bf16[2304,128]{1,0:T(8,128)(2,1)} %get-tuple-element.79), channel_id=1, source_target_pairs={{0,1},{1,2},{2,3},{4,5},{5,6},{6,7},{8,9},{9,10},{10,11},{12,13},{... | collective-permute-start | bytes 1769480 | tf_op jit(solution)/shard_map/ppermute | solution.py:782
  42.3 1.3 %collective-permute-start.9 = (bf16[2304,128]{1,0:T(8,128)(2,1)}, bf16[2304,128]{1,0:T(8,128)(2,1)S(1)}, u32[]{:S(2)}, u32[]{:S(2)}) collective-permute-start(bf16[2304,128]{1,0:T(8,128)(2,1)} %get-tuple-element.80), channel_id=1, source_target_pairs={{1,0},{2,1},{3,2},{5,4},{6,5},{7,6},{9,8},{10,9},{11,10},{13,12},{... | collective-permute-start | bytes 1769480 | tf_op jit(solution)/shard_map/ppermute | solution.py:783
  43.7 3.6 %shard_map.49 = (f32[4,8,10,8,128]{4,3,2,1,0:T(8,128)}, bf16[2,288,128]{2,1,0:T(8,128)(2,1)}, bf16[288,128]{1,0:T(8,128)(2,1)}) custom-call(bf16[1024,128]{1,0:T(8,128)(2,1)} %get-tuple-element.69.refs_0_, bf16[1024,128]{1,0:T(8,128)(2,1)} %copy-done.8, bf16[1024,128]{1,0:T(8,128)(2,1)} %copy-done.9, bf16[1024,128]{1,0:T(8,128)(2,1)} %copy-done.10, ...), custom_call_target="tpu_custom_call" | custom-call | tf_op jit(solution)/shard_map/pallas_call | solution.py:273
  47.3 1.3 %collective-permute-start.11 = (bf16[2,288,128]{2,1,0:T(8,128)(2,1)}, bf16[2,288,128]{2,1,0:T(8,128)(2,1)S(1)}, u32[]{:S(2)}, u32[]{:S(2)}) collective-permute-start(bf16[2,288,128]{2,1,0:T(8,128)(2,1)} %get-tuple-element.82), channel_id=1, source_target_pairs={{1,0},{2,1},{3,2},{5,4},{6,5},{7,6},{9,8},{10,9},{11,10},{13,12},{... | collective-permute-start | bytes 442376 | tf_op jit(solution)/shard_map/ppermute | solution.py:783
  48.5 5.2 %collective-permute-start.10 = (bf16[288,128]{1,0:T(8,128)(2,1)}, bf16[288,128]{1,0:T(8,128)(2,1)S(1)}, u32[]{:S(2)}, u32[]{:S(2)}) collective-permute-start(bf16[288,128]{1,0:T(8,128)(2,1)} %get-tuple-element.81), channel_id=1, source_target_pairs={{0,1},{1,2},{2,3},{4,5},{5,6},{6,7},{8,9},{9,10},{10,11},{12,13},{... | collective-permute-start | bytes 221192 | tf_op jit(solution)/shard_map/ppermute | solution.py:782
  53.7 8.9 %shard_map.50 = (f32[4,8,18,8,128]{4,3,2,1,0:T(8,128)}, f32[4,8,22,8,128]{4,3,2,1,0:T(8,128)}) custom-call(f32[4,16,18,8,128]{4,3,2,1,0:T(8,128)} %get-tuple-element.55.refs_0_.refs_3_.refs_7_, f32[4,8,10,8,128]{4,3,2,1,0:T(8,128)} %get-tuple-element.77.refs_1_.refs_4_.refs_2_), custom_call_target="tpu_custom_call" | custom-call | tf_op jit(solution)/shard_map/pallas_call | solution.py:746
  64.4 9.5 %shard_map.51 = (f32[4,8,18,8,128]{4,3,2,1,0:T(8,128)}, bf16[2304,128]{1,0:T(8,128)(2,1)}, bf16[2304,128]{1,0:T(8,128)(2,1)}) custom-call(f32[4,16,18,8,128]{4,3,2,1,0:T(8,128)} %get-tuple-element.55.refs_0_.refs_3_.refs_7_, f32[4,8,22,8,128]{4,3,2,1,0:T(8,128)} %get-tuple-element.78.refs_1_, bf16[2304,128]{1,0:T(8,128)(2,1)} %copy-done, ...), custom_call_target="tpu_custom_call" | custom-call | tf_op jit(solution)/shard_map/pallas_call | solution.py:765
  73.9 3.6 %collective-permute-start.12 = (bf16[2304,128]{1,0:T(8,128)(2,1)}, bf16[2304,128]{1,0:T(8,128)(2,1)S(1)}, u32[]{:S(2)}, u32[]{:S(2)}) collective-permute-start(bf16[2304,128]{1,0:T(8,128)(2,1)} %get-tuple-element.86), channel_id=1, source_target_pairs={{0,1},{1,2},{2,3},{4,5},{5,6},{6,7},{8,9},{9,10},{10,11},{12,13},{... | collective-permute-start | bytes 1769480 | tf_op jit(solution)/shard_map/ppermute | solution.py:782
  77.5 1.3 %collective-permute-start.13 = (bf16[2304,128]{1,0:T(8,128)(2,1)}, bf16[2304,128]{1,0:T(8,128)(2,1)S(1)}, u32[]{:S(2)}, u32[]{:S(2)}) collective-permute-start(bf16[2304,128]{1,0:T(8,128)(2,1)} %get-tuple-element.87), channel_id=1, source_target_pairs={{1,0},{2,1},{3,2},{5,4},{6,5},{7,6},{9,8},{10,9},{11,10},{13,12},{... | collective-permute-start | bytes 1769480 | tf_op jit(solution)/shard_map/ppermute | solution.py:783
  78.8 10.8 %shard_map.52 = (f32[4,8,296,128]{3,2,1,0:T(8,128)}, f32[4,8,22,8,128]{4,3,2,1,0:T(8,128)}) custom-call(f32[4,8,18,8,128]{4,3,2,1,0:T(8,128)} %get-tuple-element.84.refs_0_, f32[4,8,18,8,128]{4,3,2,1,0:T(8,128)} %get-tuple-element.83.refs_1_.refs_0_, f32[4,8,10,8,128]{4,3,2,1,0:T(8,128)} %get-tuple-element.77.refs_1_.refs_4_.refs_2_, ...), custom_call_target="tpu_custom_call" | custom-call | tf_op jit(solution)/shard_map/pallas_call | solution.py:746
  89.8 4.0 %collective-permute-done.13.refs_3_ = bf16[2304,128]{1,0:T(8,128)(2,1)S(1)} collective-permute-done((bf16[2304,128]{1,0:T(8,128)(2,1)}, bf16[2304,128]{1,0:T(8,128)(2,1)S(1)}, u32[]{:S(2)}, u32[]{:S(2)}) %collective-permute-start.13) | collective-permute-done | bytes 589856 | tf_op jit(solution)/shard_map/ppermute | solution.py:783
  93.9 0.8 copy-done.5
  94.7 12.8 %shard_map.53 = f32[4,2048,128]{2,1,0:T(8,128)} custom-call(f32[4,8,18,8,128]{4,3,2,1,0:T(8,128)} %get-tuple-element.83.refs_1_.refs_0_, f32[4,8,22,8,128]{4,3,2,1,0:T(8,128)} %get-tuple-element.85.refs_1_, bf16[2304,128]{1,0:T(8,128)(2,1)} %copy-done.4, bf16[2304,128]{1,0:T(8,128)(2,1)} %copy-done.5, ...), custom_call_target="tpu_custom_call" | custom-call | tf_op jit(solution)/shard_map/pallas_call | solution.py:756
  (42 shorter events, 4.2 us)
Async XLA Ops:
  3.9 10.1 %collective-permute-start = (bf16[768,128]{1,0:T(8,128)(2,1)}, bf16[768,128]{1,0:T(8,128)(2,1)S(1)}, u32[]{:S(2)}, u32[]{:S(2)}) collective-permute-start(bf16[768,128]{1,0:T(8,128)(2,1)} %get-tuple-element.47), channel_id=1, source_target_pairs={{0,4},{4,8},{8,12},{12,16},{16,20},{20,24},{24,28},{1,5},{5,9},{9,... | collective-permute-start | bytes 589832 | tf_op jit(solution)/shard_map/ppermute | solution.py:782
  6.2 7.7 %collective-permute-start.1 = (bf16[768,128]{1,0:T(8,128)(2,1)}, bf16[768,128]{1,0:T(8,128)(2,1)S(1)}, u32[]{:S(2)}, u32[]{:S(2)}) collective-permute-start(bf16[768,128]{1,0:T(8,128)(2,1)} %get-tuple-element.48), channel_id=1, source_target_pairs={{4,0},{8,4},{12,8},{16,12},{20,16},{24,20},{28,24},{5,1},{9,5},{13... | collective-permute-start | bytes 589832 | tf_op jit(solution)/shard_map/ppermute | solution.py:783
  7.5 31.1 %collective-permute-start.2 = (bf16[1024,128]{1,0:T(8,128)(2,1)}, bf16[1024,128]{1,0:T(8,128)(2,1)S(1)}, u32[]{:S(2)}, u32[]{:S(2)}) collective-permute-start(bf16[1024,128]{1,0:T(8,128)(2,1)} %get-tuple-element.57), channel_id=1, source_target_pairs={{0,1},{1,2},{2,3},{3,0},{4,5},{5,6},{6,7},{7,4},{8,9},{9,10},{10,1... | collective-permute-start | bytes 786440 | tf_op jit(solution)/shard_map/ppermute | solution.py:792
  10.0 28.7 %collective-permute-start.3 = (bf16[1024,128]{1,0:T(8,128)(2,1)}, bf16[1024,128]{1,0:T(8,128)(2,1)S(1)}, u32[]{:S(2)}, u32[]{:S(2)}) collective-permute-start(bf16[1024,128]{1,0:T(8,128)(2,1)} %get-tuple-element.58), channel_id=1, source_target_pairs={{0,2},{1,3},{2,0},{3,1},{4,6},{5,7},{6,4},{7,5},{8,10},{9,11},{10,... | collective-permute-start | bytes 786440 | tf_op jit(solution)/shard_map/ppermute | solution.py:792
  12.6 26.1 %collective-permute-start.4 = (bf16[1024,128]{1,0:T(8,128)(2,1)}, bf16[1024,128]{1,0:T(8,128)(2,1)S(1)}, u32[]{:S(2)}, u32[]{:S(2)}) collective-permute-start(bf16[1024,128]{1,0:T(8,128)(2,1)} %get-tuple-element.59), channel_id=1, source_target_pairs={{0,3},{1,0},{2,1},{3,2},{4,7},{5,4},{6,5},{7,6},{8,11},{9,8},{10,9... | collective-permute-start | bytes 786440 | tf_op jit(solution)/shard_map/ppermute | solution.py:792
  17.0 12.6 %copy-start.14 = (bf16[128,128]{1,0:T(8,128)(2,1)S(1)}, bf16[128,128]{1,0:T(8,128)(2,1)}, u32[]{:S(2)}) copy-start(bf16[128,128]{1,0:T(8,128)(2,1)} %get-tuple-element.66) | copy-start | bytes 98308
  17.0 12.6 %collective-permute-start.5 = (bf16[128,128]{1,0:T(8,128)(2,1)}, bf16[128,128]{1,0:T(8,128)(2,1)S(1)}, u32[]{:S(2)}, u32[]{:S(2)}) collective-permute-start(bf16[128,128]{1,0:T(8,128)(2,1)} %get-tuple-element.61), channel_id=1, source_target_pairs={{0,1},{1,2},{2,3},{3,0},{4,5},{5,6},{6,7},{7,4},{8,9},{9,10},{10,1... | collective-permute-start | bytes 98312 | tf_op jit(solution)/shard_map/ppermute | solution.py:792
  17.7 20.7 %collective-permute-start.6 = (bf16[128,128]{1,0:T(8,128)(2,1)}, bf16[128,128]{1,0:T(8,128)(2,1)S(1)}, u32[]{:S(2)}, u32[]{:S(2)}) collective-permute-start(bf16[128,128]{1,0:T(8,128)(2,1)} %get-tuple-element.62), channel_id=1, source_target_pairs={{0,2},{1,3},{2,0},{3,1},{4,6},{5,7},{6,4},{7,5},{8,10},{9,11},{10,... | collective-permute-start | bytes 98312 | tf_op jit(solution)/shard_map/ppermute | solution.py:792
  29.6 14.0 %copy-start.11 = (bf16[128,128]{1,0:T(8,128)(2,1)}, bf16[128,128]{1,0:T(8,128)(2,1)S(1)}, u32[]{:S(2)}) copy-start(bf16[128,128]{1,0:T(8,128)(2,1)S(1)} %collective-permute-done.5.refs_5_) | copy-start | bytes 98308
  29.6 9.0 %collective-permute-start.7 = (bf16[128,128]{1,0:T(8,128)(2,1)S(1)}, bf16[128,128]{1,0:T(8,128)(2,1)S(1)}, u32[]{:S(2)}, u32[]{:S(2)}) collective-permute-start(bf16[128,128]{1,0:T(8,128)(2,1)S(1)} %copy-done.14), channel_id=1, source_target_pairs={{0,3},{1,0},{2,1},{3,2},{4,7},{5,4},{6,5},{7,6},{8,11},{9,8},{10,9... | collective-permute-start | bytes 98312 | tf_op jit(solution)/shard_map/ppermute | solution.py:792
  38.3 5.3 %copy-start.12 = (bf16[128,128]{1,0:T(8,128)(2,1)}, bf16[128,128]{1,0:T(8,128)(2,1)S(1)}, u32[]{:S(2)}) copy-start(bf16[128,128]{1,0:T(8,128)(2,1)S(1)} %collective-permute-done.6.refs_6_) | copy-start | bytes 98308
  38.6 5.0 %copy-start.13 = (bf16[128,128]{1,0:T(8,128)(2,1)}, bf16[128,128]{1,0:T(8,128)(2,1)S(1)}, u32[]{:S(2)}) copy-start(bf16[128,128]{1,0:T(8,128)(2,1)S(1)} %collective-permute-done.7.refs_7_) | copy-start | bytes 98308
  38.6 5.0 %copy-start.8 = (bf16[1024,128]{1,0:T(8,128)(2,1)}, bf16[1024,128]{1,0:T(8,128)(2,1)S(1)}, u32[]{:S(2)}) copy-start(bf16[1024,128]{1,0:T(8,128)(2,1)S(1)} %collective-permute-done.2.refs_1_) | copy-start | bytes 786436
  38.6 5.0 %copy-start.9 = (bf16[1024,128]{1,0:T(8,128)(2,1)}, bf16[1024,128]{1,0:T(8,128)(2,1)S(1)}, u32[]{:S(2)}) copy-start(bf16[1024,128]{1,0:T(8,128)(2,1)S(1)} %collective-permute-done.3.refs_2_) | copy-start | bytes 786436
  38.7 5.0 %copy-start.10 = (bf16[1024,128]{1,0:T(8,128)(2,1)}, bf16[1024,128]{1,0:T(8,128)(2,1)S(1)}, u32[]{:S(2)}) copy-start(bf16[1024,128]{1,0:T(8,128)(2,1)S(1)} %collective-permute-done.4.refs_3_) | copy-start | bytes 786436
  38.7 24.7 %collective-permute-start.8 = (bf16[2304,128]{1,0:T(8,128)(2,1)}, bf16[2304,128]{1,0:T(8,128)(2,1)S(1)}, u32[]{:S(2)}, u32[]{:S(2)}) collective-permute-start(bf16[2304,128]{1,0:T(8,128)(2,1)} %get-tuple-element.79), channel_id=1, source_target_pairs={{0,1},{1,2},{2,3},{4,5},{5,6},{6,7},{8,9},{9,10},{10,11},{12,13},{... | collective-permute-start | bytes 1769480 | tf_op jit(solution)/shard_map/ppermute | solution.py:782
  42.3 21.0 %collective-permute-start.9 = (bf16[2304,128]{1,0:T(8,128)(2,1)}, bf16[2304,128]{1,0:T(8,128)(2,1)S(1)}, u32[]{:S(2)}, u32[]{:S(2)}) collective-permute-start(bf16[2304,128]{1,0:T(8,128)(2,1)} %get-tuple-element.80), channel_id=1, source_target_pairs={{1,0},{2,1},{3,2},{5,4},{6,5},{7,6},{9,8},{10,9},{11,10},{13,12},{... | collective-permute-start | bytes 1769480 | tf_op jit(solution)/shard_map/ppermute | solution.py:783
  47.3 16.1 %collective-permute-start.11 = (bf16[2,288,128]{2,1,0:T(8,128)(2,1)}, bf16[2,288,128]{2,1,0:T(8,128)(2,1)S(1)}, u32[]{:S(2)}, u32[]{:S(2)}) collective-permute-start(bf16[2,288,128]{2,1,0:T(8,128)(2,1)} %get-tuple-element.82), channel_id=1, source_target_pairs={{1,0},{2,1},{3,2},{5,4},{6,5},{7,6},{9,8},{10,9},{11,10},{13,12},{... | collective-permute-start | bytes 442376 | tf_op jit(solution)/shard_map/ppermute | solution.py:783
  48.5 14.1 %collective-permute-start.10 = (bf16[288,128]{1,0:T(8,128)(2,1)}, bf16[288,128]{1,0:T(8,128)(2,1)S(1)}, u32[]{:S(2)}, u32[]{:S(2)}) collective-permute-start(bf16[288,128]{1,0:T(8,128)(2,1)} %get-tuple-element.81), channel_id=1, source_target_pairs={{0,1},{1,2},{2,3},{4,5},{5,6},{6,7},{8,9},{9,10},{10,11},{12,13},{... | collective-permute-start | bytes 221192 | tf_op jit(solution)/shard_map/ppermute | solution.py:782
  63.3 0.9 copy-start
  63.3 1.0 copy-start.1
  73.9 15.9 %collective-permute-start.12 = (bf16[2304,128]{1,0:T(8,128)(2,1)}, bf16[2304,128]{1,0:T(8,128)(2,1)S(1)}, u32[]{:S(2)}, u32[]{:S(2)}) collective-permute-start(bf16[2304,128]{1,0:T(8,128)(2,1)} %get-tuple-element.86), channel_id=1, source_target_pairs={{0,1},{1,2},{2,3},{4,5},{5,6},{6,7},{8,9},{9,10},{10,11},{12,13},{... | collective-permute-start | bytes 1769480 | tf_op jit(solution)/shard_map/ppermute | solution.py:782
  77.5 16.3 %collective-permute-start.13 = (bf16[2304,128]{1,0:T(8,128)(2,1)}, bf16[2304,128]{1,0:T(8,128)(2,1)S(1)}, u32[]{:S(2)}, u32[]{:S(2)}) collective-permute-start(bf16[2304,128]{1,0:T(8,128)(2,1)} %get-tuple-element.87), channel_id=1, source_target_pairs={{1,0},{2,1},{3,2},{5,4},{6,5},{7,6},{9,8},{10,9},{11,10},{13,12},{... | collective-permute-start | bytes 1769480 | tf_op jit(solution)/shard_map/ppermute | solution.py:783
  89.8 4.0 %copy-start.4 = (bf16[2304,128]{1,0:T(8,128)(2,1)}, bf16[2304,128]{1,0:T(8,128)(2,1)S(1)}, u32[]{:S(2)}) copy-start(bf16[2304,128]{1,0:T(8,128)(2,1)S(1)} %collective-permute-done.12.refs_2_) | copy-start | bytes 1769476
  (5 other events, 3.5 us)
where the time goes:
time: 108 us
  Pallas kernels  57.2 us (53%)
  starting transfers between devices  27.8 us (26%)
  waiting for transfers between devices  19 us (18%)
  local copies, waits for them, and re-layouts  3.21 us (3%)
    pallas_call x2, Pallas kernels, advance(): call(functools.partial(inner_kernel, factors, final), [shape_of(*inner_re...  19.7 us
    ppermute x4, starting transfers between devices, exchange(): lax.ppermute(to_next, axis, neighbours(axis, True))  14.8 us
    ppermute x6, waiting for transfers between devices, to_owners(): moved.append(lax.ppermute(pieces[shift], 'wa', ring))  14.2 us
    pallas_call x1, Pallas kernels, advance(): call(functools.partial(outer_kernel, factors, final), [shape_of(4, (run *...  12.8 us
    pallas_call x1, Pallas kernels, advance(): call(functools.partial(outer_kernel, factors, final), [shape_of(*half_blo...  9.54 us
    ppermute x6, starting transfers between devices, to_owners(): moved.append(lax.ppermute(pieces[shift], 'wa', ring))  7.82 us
    pallas_call x1, Pallas kernels, widen(): call(widen_kernel, [shape_of(4, height, run, 8, 128), layer, layer], [hbm...  6.03 us
    ppermute x4, starting transfers between devices, exchange(): lax.ppermute(to_previous, axis, neighbours(axis, False))  5.16 us
  transfers between devices with their start and end apart: 14, of which 6 were waited for; matrix products, arithmetic and copies ran while one was open for 0% of the time, Pallas kernels for 29%

commit v1 on v0

--- a/solution.py
+++ b/solution.py
@@ -261,10 +261,13 @@
 
         lax.fori_loop(0, levels, body, 0)
         rows = run * 8
-        at = pl.ds(f * rows, rows)
-        send_high[at, :] = out[f, levels - 1, :run].reshape(rows, 128).astype(bf16)
+        send_high[pl.ds(f * rows, rows), :] = (
+            out[f, levels - 1, :run].reshape(rows, 128).astype(bf16)
+        )
         for k in range(2):
-            send_low[k, at, :] = out[f, k, :run].reshape(rows, 128).astype(bf16)
+            send_low[pl.ds((4 * k + f) * rows, rows), :] = (
+                out[f, k, :run].reshape(rows, 128).astype(bf16)
+            )
 
 
 def spread(tiles, tails, y_index, y_weight, columns, levels, width):
@@ -274,7 +277,7 @@
         functools.partial(spread_kernel, devices, width),
         [
             shape_of(4, levels, run + 1, 8, 128),
-            shape_of(2, 4 * run * 8, 128, dtype=bf16),
+            shape_of(2 * 4 * run * 8, 128, dtype=bf16),
             shape_of(4 * run * 8, 128, dtype=bf16),
         ],
         [vmem] * (2 * devices + 2),
@@ -582,16 +585,26 @@
 
 
 def outer_kernel(factors, final, *refs):
-    state, edges, low, high, flow_in, below, above = refs[:7]
+    state, edges, low_in, high_in, flow_in, below_in, above_in = refs[:7]
     if final:
-        anchor, q_low, q_high, part, out = refs[7:12]
+        anchor, q_low_in, q_high_in, part, out = refs[7:12]
         scratch = refs[12:]
         base, q_sem, part_sem = scratch[-3:]
+        halos_in = (low_in, high_in, q_low_in, q_high_in, below_in, above_in)
     else:
         out, send_low, send_high = refs[7:10]
         scratch = refs[10:]
         base = None
-    fields, middle, coeffs, result, slopes, flow, in_sem, out_sem, flow_sem = scratch[:9]
+        halos_in = (low_in, high_in, below_in, above_in)
+    fields, middle, coeffs, result, slopes, flow, in_sem, out_sem, flow_sem, halos, halo_sem = (
+        scratch[:11]
+    )
+    halo_copies = [
+        pltpu.make_async_copy(ref, halos.at[index, pl.ds(0, ref.shape[0])], halo_sem.at[index])
+        for index, ref in enumerate(halos_in)
+    ]
+    for copy in halo_copies:
+        copy.start()
     run = coeffs.shape[2]
     levels = flow_in.shape[1]
     height = fields.shape[1] - 2 * layers
@@ -631,24 +644,34 @@
         part_copy = pltpu.make_async_copy(part, result, part_sem)
         part_copy.start()
 
-    def layer(ref, f, z):
-        value = ref[pl.ds((f * layers + z) * rows, rows), :].astype(f32)
+    for copy in halo_copies:
+        copy.wait()
+
+    def layer(index, f, z):
+        value = halos[index, pl.ds((f * layers + z) * rows, rows), :].astype(f32)
         return [value[8 * i : 8 * i + 8] for i in range(run)]
 
     for f in range(4):
         for z in range(layers):
-            put_plane(fields, f, z, layer(low, f, z))
-            put_plane(fields, f, layers + height + z, layer(high, f, z))
+            put_plane(fields, f, z, layer(0, f, z))
+            put_plane(fields, f, layers + height + z, layer(1, f, z))
         if final:
             for z in range(2):
-                for target, ref, from_z in ((z, q_low, layers - 2 + z), (height + 2 + z, q_high, z)):
-                    for i, value in enumerate(layer(ref, f, from_z)):
+                for target, index, from_z in ((z, 2, layers - 2 + z), (height + 2 + z, 3, z)):
+                    for i, value in enumerate(layer(index, f, from_z)):
                         base[f, target, i] = value
     flow_copy.wait()
     half_run = run // 2
     for f in range(4):
-        at = pl.ds(f * half_run * 8, half_run * 8)
-        under, over, over_next = (below[at, :], above[0, at, :], above[1, at, :])
+        flow_rows = half_run * 8
+        under, over, over_next = [
+            halos[
+                len(halos_in) - 2 + side,
+                pl.ds((4 * k + f) * flow_rows, flow_rows),
+                :,
+            ]
+            for side, k in ((0, 0), (1, 0), (1, 1))
+        ]
         for j in range(half_run):
             piece = slice(8 * j, 8 * j + 8)
             values = (
@@ -660,8 +683,6 @@
                 flow[f, level, j] = value
                 if j == 0:
                     flow[f, level, half_run] = down(value)
-    if final:
-        part_copy.wait()
     sweep = Sweep(
         fields, middle, coeffs, slopes, flow, result, base, factors, lambda step: 8 * (step // 4)
     )
@@ -691,6 +712,12 @@
         @pl.when(upper & (half == 1))
         def _():
             sweep.clear_first(9)
+
+        if final:
+
+            @pl.when(half == 0)
+            def _():
+                part_copy.wait()
 
         for k in range(2):
             sweep.last_slopes(6 * half + k, 2 + k)
@@ -722,8 +749,12 @@
 
 def advance(height, run, halo, flow, factors, state=None, parts=None, anchor=None, anchor_halo=None):
     final = anchor is not None
-    flow, below, above = flow
     pairs = height // 2
+    flow, *flow_halo = flow
+    halo_scratch = [
+        pltpu.VMEM((6 if final else 4, halo[0].shape[0], 128), bf16),
+        pltpu.SemaphoreType.DMA((6,)),
+    ]
     natural = (4, 8, run * height + pad, 128)
     half_block = (4, height // 2, run, 8, 128)
     inner_result = natural if final else half_block
@@ -750,15 +781,18 @@
         [hbm, hbm],
         common + sems + ([base, pltpu.SemaphoreType.DMA((pairs,))] if final else []),
     )(*operands)
-    operands = [parts[1] if final else state, edges, *halo, flow, below, above]
-    in_specs = [hbm, hbm, vmem, vmem, hbm, vmem, vmem]
+    operands = [parts[1] if final else state, edges, *halo, flow, *flow_halo]
+    in_specs = [hbm] * 7
     if final:
         (out,) = call(
             functools.partial(outer_kernel, factors, final),
             [shape_of(4, (run * 8 - 2 * reach) * height, 128)],
-            in_specs + [hbm, vmem, vmem, hbm],
+            in_specs + [hbm] * 4,
             [hbm],
-            common + sems + [base, pltpu.SemaphoreType.DMA((2,)), pltpu.SemaphoreType.DMA],
+            common
+            + sems
+            + halo_scratch
+            + [base, pltpu.SemaphoreType.DMA((2,)), pltpu.SemaphoreType.DMA],
         )(*operands, anchor, *anchor_halo, inner)
         return out
     layer = shape_of(4 * layers * run * 8, 128, dtype=bf16)
@@ -767,7 +801,7 @@
         [shape_of(*half_block), layer, layer],
         in_specs,
         [hbm, vmem, vmem],
-        common + sems,
+        common + sems + halo_scratch,
     )(*operands)
     return ((inner, outer), send_low, send_high)
 
@@ -803,7 +837,7 @@
     tails = cut_tails(before, after, skip, levels, devices)
     before, after, *tails = lax.optimization_barrier((before, after, *tails))
     state, send_low, send_high = widen(acoustic_state, before, after)
-    send_low, send_high, *late = lax.optimization_barrier((send_low, send_high, *tails[3:]))
+    tiles[1], *late = lax.optimization_barrier((tiles[1], *tails[3:]))
     tails = to_owners(tails[:3] + late)
     tiles, tails, send_low, send_high = lax.optimization_barrier(
         (tiles, tails, send_low, send_high)
@@ -812,8 +846,7 @@
     flow, low, high = spread(
         tiles, tails, y_index, y_weight, columns, levels // devices, width
     )
-    below, above = exchange(high, low, "wa")
-    flow = (flow, below, above)
+    flow = (flow, *exchange(high, low, "wa"))
     height, run = state.shape[1:3]
     parts, send_low, send_high = advance(height, run, halo, flow, (1 / 4, 1 / 3), state=state)
     half_halo = exchange(send_high, send_low, "wa")

time: 108 us -> 99.6 us (0.922)
  waiting for transfers between devices: 19 us -> 12.2 us
  Pallas kernels: 57.2 us -> 54.4 us
  starting transfers between devices: 27.8 us -> 29.5 us
    ppermute x6, waiting for transfers between devices: 14.2 us -> 4.78 us  [to_owners(): moved.append(lax.ppermute(pieces[shift], 'wa', ring))]
    ppermute x6, starting transfers between devices: 7.82 us -> 10.9 us  [to_owners(): moved.append(lax.ppermute(pieces[shift], 'wa', ring))]
    ppermute x4, waiting for transfers between devices: 4.71 us -> 7.44 us  [exchange(): lax.ppermute(to_previous, axis, neighbours(axis, False))]
    pallas_call x1, Pallas kernels: 12.8 us -> 10.8 us  [advance(): call(functools.partial(outer_kernel, factors, final), [shape_of(4, (run *...]
    ppermute x4, starting transfers between devices: 14.8 us -> 13.4 us  [exchange(): lax.ppermute(to_next, axis, neighbours(axis, True))]
    unnamed x30 -> x28, local copies, waits for them, and re-layouts: 3.21 us -> 2.54 us
  transfers between devices with their start and end apart: 14 -> 14, of which waited for: 6 -> 3; matrix products, arithmetic and copies ran while one was open for 0% -> 0% of each run, Pallas kernels for 29% -> 31%
where the time goes in v1:
time: 99.6 us; the launch traced here: 99.2 us
  Pallas kernels  54.4 us (55%)
  starting transfers between devices  29.5 us (30%)
  waiting for transfers between devices  12.2 us (12%)
  local copies, waits for them, and re-layouts  2.54 us (3%)
    pallas_call x2, Pallas kernels, advance(): call(functools.partial(inner_kernel, factors, final), [shape_of(*inner_re...  19.8 us
    ppermute x4, starting transfers between devices, exchange(): lax.ppermute(to_next, axis, neighbours(axis, True))  13.4 us
    ppermute x6, starting transfers between devices, to_owners(): moved.append(lax.ppermute(pieces[shift], 'wa', ring))  10.9 us
    pallas_call x1, Pallas kernels, advance(): call(functools.partial(outer_kernel, factors, final), [shape_of(4, (run *...  10.8 us
    pallas_call x1, Pallas kernels, advance(): call(functools.partial(outer_kernel, factors, final), [shape_of(*half_blo...  8.73 us
    ppermute x4, waiting for transfers between devices, exchange(): lax.ppermute(to_previous, axis, neighbours(axis, False))  7.44 us
    pallas_call x1, Pallas kernels, widen(): call(widen_kernel, [shape_of(4, height, run, 8, 128), layer, layer], [hbm...  6.05 us
    ppermute x4, starting transfers between devices, exchange(): lax.ppermute(to_previous, axis, neighbours(axis, False))  5.16 us
  transfers between devices with their start and end apart: 14, of which 3 were waited for; matrix products, arithmetic and copies ran while one was open for 0% of the time, Pallas kernels for 31%

profile of v1, /device:TPU:0, one launch (start us, length us, event | category | flops | bytes accessed | tf_op | source)
XLA Modules:
  0.0 99.2 jit_solution(6635317045802476324)
XLA Ops:
  0.0 3.8 %shard_map.46 = (bf16[1024,128]{1,0:T(8,128)(2,1)}, bf16[1024,128]{1,0:T(8,128)(2,1)}, bf16[1024,128]{1,0:T(8,128)(2,1)}, bf16[1024,128]{1,0:T(8,128)(2,1)}, bf1...) custom-call(bf16[4,64,32,64]{3,2,1,0:T(8,128)(2,1)} %les.1, f32[4,128,16,128]{3,2,1,0:T(8,128)} %state.1), custom_call_target="tpu_custom_call" | custom-call | tf_op jit(solution)/shard_map/pallas_call | solution.py:99
  3.8 3.1 %collective-permute-start.2 = (bf16[1024,128]{1,0:T(8,128)(2,1)}, bf16[1024,128]{1,0:T(8,128)(2,1)S(1)}, u32[]{:S(2)}, u32[]{:S(2)}) collective-permute-start(bf16[1024,128]{1,0:T(8,128)(2,1)} %get-tuple-element.56), channel_id=1, source_target_pairs={{0,1},{1,2},{2,3},{3,0},{4,5},{5,6},{6,7},{7,4},{8,9},{9,10},{10,1... | collective-permute-start | bytes 786440 | tf_op jit(solution)/shard_map/ppermute | solution.py:826
  6.9 2.6 %collective-permute-start.3 = (bf16[1024,128]{1,0:T(8,128)(2,1)}, bf16[1024,128]{1,0:T(8,128)(2,1)S(1)}, u32[]{:S(2)}, u32[]{:S(2)}) collective-permute-start(bf16[1024,128]{1,0:T(8,128)(2,1)} %get-tuple-element.59), channel_id=1, source_target_pairs={{0,2},{1,3},{2,0},{3,1},{4,6},{5,7},{6,4},{7,5},{8,10},{9,11},{10,... | collective-permute-start | bytes 786440 | tf_op jit(solution)/shard_map/ppermute | solution.py:826
  9.5 1.3 %collective-permute-start.4 = (bf16[1024,128]{1,0:T(8,128)(2,1)}, bf16[1024,128]{1,0:T(8,128)(2,1)S(1)}, u32[]{:S(2)}, u32[]{:S(2)}) collective-permute-start(bf16[1024,128]{1,0:T(8,128)(2,1)} %get-tuple-element.60), channel_id=1, source_target_pairs={{0,3},{1,0},{2,1},{3,2},{4,7},{5,4},{6,5},{7,6},{8,11},{9,8},{10,9... | collective-permute-start | bytes 786440 | tf_op jit(solution)/shard_map/ppermute | solution.py:826
  10.9 1.3 %collective-permute-start = (bf16[768,128]{1,0:T(8,128)(2,1)}, bf16[768,128]{1,0:T(8,128)(2,1)S(1)}, u32[]{:S(2)}, u32[]{:S(2)}) collective-permute-start(bf16[768,128]{1,0:T(8,128)(2,1)} %get-tuple-element.46), channel_id=1, source_target_pairs={{0,4},{4,8},{8,12},{12,16},{16,20},{20,24},{24,28},{1,5},{5,9},{9,... | collective-permute-start | bytes 589832 | tf_op jit(solution)/shard_map/ppermute | solution.py:816
  12.2 1.3 %collective-permute-start.1 = (bf16[768,128]{1,0:T(8,128)(2,1)}, bf16[768,128]{1,0:T(8,128)(2,1)S(1)}, u32[]{:S(2)}, u32[]{:S(2)}) collective-permute-start(bf16[768,128]{1,0:T(8,128)(2,1)} %get-tuple-element.47), channel_id=1, source_target_pairs={{4,0},{8,4},{12,8},{16,12},{20,16},{24,20},{28,24},{5,1},{9,5},{13... | collective-permute-start | bytes 589832 | tf_op jit(solution)/shard_map/ppermute | solution.py:817
  13.5 3.9 %collective-permute-done.1.after = bf16[768,128]{1,0:T(8,128)(2,1)S(1)} collective-permute-done((bf16[768,128]{1,0:T(8,128)(2,1)}, bf16[768,128]{1,0:T(8,128)(2,1)S(1)}, u32[]{:S(2)}, u32[]{:S(2)}) %collective-permute-start.1) | collective-permute-done | bytes 196640 | tf_op jit(solution)/shard_map/ppermute | solution.py:817
  18.1 1.7 %shard_map.47 = (bf16[128,128]{1,0:T(8,128)(2,1)}, bf16[128,128]{1,0:T(8,128)(2,1)}, bf16[128,128]{1,0:T(8,128)(2,1)}, bf16[128,128]{1,0:T(8,128)(2,1)}) custom-call(bf16[768,128]{1,0:T(8,128)(2,1)} %copy-done.2, bf16[768,128]{1,0:T(8,128)(2,1)} %copy-done.3), custom_call_target="tpu_custom_call" | custom-call | tf_op jit(solution)/shard_map/pallas_call | solution.py:130
  20.8 2.9 %collective-permute-start.7 = (bf16[128,128]{1,0:T(8,128)(2,1)}, bf16[128,128]{1,0:T(8,128)(2,1)S(1)}, u32[]{:S(2)}, u32[]{:S(2)}) collective-permute-start(bf16[128,128]{1,0:T(8,128)(2,1)} %get-tuple-element.64), channel_id=1, source_target_pairs={{0,3},{1,0},{2,1},{3,2},{4,7},{5,4},{6,5},{7,6},{8,11},{9,8},{10,9... | collective-permute-start | bytes 98312 | tf_op jit(solution)/shard_map/ppermute | solution.py:826
  23.7 6.0 %shard_map.48 = (f32[4,16,18,8,128]{4,3,2,1,0:T(8,128)}, bf16[2304,128]{1,0:T(8,128)(2,1)}, bf16[2304,128]{1,0:T(8,128)(2,1)}) custom-call(f32[4,2048,128]{2,1,0:T(8,128)} %bitcast.4, bf16[768,128]{1,0:T(8,128)(2,1)} %copy-done.2, bf16[768,128]{1,0:T(8,128)(2,1)} %copy-done.3), custom_call_target="tpu_custom_call" | custom-call | tf_op jit(solution)/shard_map/pallas_call | solution.py:199
  29.8 4.8 %collective-permute-done.6.refs_6_ = bf16[128,128]{1,0:T(8,128)(2,1)S(1)} collective-permute-done((bf16[128,128]{1,0:T(8,128)(2,1)}, bf16[128,128]{1,0:T(8,128)(2,1)S(1)}, u32[]{:S(2)}, u32[]{:S(2)}) %collective-permute-start.6) | collective-permute-done | bytes 32800 | tf_op jit(solution)/shard_map/ppermute | solution.py:826
  34.6 3.1 %collective-permute-start.8 = (bf16[2304,128]{1,0:T(8,128)(2,1)}, bf16[2304,128]{1,0:T(8,128)(2,1)S(1)}, u32[]{:S(2)}, u32[]{:S(2)}) collective-permute-start(bf16[2304,128]{1,0:T(8,128)(2,1)} %get-tuple-element.77), channel_id=1, source_target_pairs={{0,1},{1,2},{2,3},{4,5},{5,6},{6,7},{8,9},{9,10},{10,11},{12,13},{... | collective-permute-start | bytes 1769480 | tf_op jit(solution)/shard_map/ppermute | solution.py:816
  37.7 1.3 %collective-permute-start.9 = (bf16[2304,128]{1,0:T(8,128)(2,1)}, bf16[2304,128]{1,0:T(8,128)(2,1)S(1)}, u32[]{:S(2)}, u32[]{:S(2)}) collective-permute-start(bf16[2304,128]{1,0:T(8,128)(2,1)} %get-tuple-element.78), channel_id=1, source_target_pairs={{1,0},{2,1},{3,2},{5,4},{6,5},{7,6},{9,8},{10,9},{11,10},{13,12},{... | collective-permute-start | bytes 1769480 | tf_op jit(solution)/shard_map/ppermute | solution.py:817
  39.0 3.6 %shard_map.49 = (f32[4,8,10,8,128]{4,3,2,1,0:T(8,128)}, bf16[576,128]{1,0:T(8,128)(2,1)}, bf16[288,128]{1,0:T(8,128)(2,1)}) custom-call(bf16[1024,128]{1,0:T(8,128)(2,1)} %get-tuple-element.67.refs_0_, bf16[1024,128]{1,0:T(8,128)(2,1)} %copy-done.8, bf16[1024,128]{1,0:T(8,128)(2,1)} %copy-done.9, bf16[1024,128]{1,0:T(8,128)(2,1)} %copy-done.10, ...), custom_call_target="tpu_custom_call" | custom-call | tf_op jit(solution)/shard_map/pallas_call | solution.py:276
  42.6 1.3 %collective-permute-start.11 = (bf16[576,128]{1,0:T(8,128)(2,1)}, bf16[576,128]{1,0:T(8,128)(2,1)S(1)}, u32[]{:S(2)}, u32[]{:S(2)}) collective-permute-start(bf16[576,128]{1,0:T(8,128)(2,1)} %get-tuple-element.80), channel_id=1, source_target_pairs={{1,0},{2,1},{3,2},{5,4},{6,5},{7,6},{9,8},{10,9},{11,10},{13,12},{... | collective-permute-start | bytes 442376 | tf_op jit(solution)/shard_map/ppermute | solution.py:817
  43.9 5.2 %collective-permute-start.10 = (bf16[288,128]{1,0:T(8,128)(2,1)}, bf16[288,128]{1,0:T(8,128)(2,1)S(1)}, u32[]{:S(2)}, u32[]{:S(2)}) collective-permute-start(bf16[288,128]{1,0:T(8,128)(2,1)} %get-tuple-element.79), channel_id=1, source_target_pairs={{0,1},{1,2},{2,3},{4,5},{5,6},{6,7},{8,9},{9,10},{10,11},{12,13},{... | collective-permute-start | bytes 221192 | tf_op jit(solution)/shard_map/ppermute | solution.py:816
  49.1 8.9 %shard_map.50 = (f32[4,8,18,8,128]{4,3,2,1,0:T(8,128)}, f32[4,8,22,8,128]{4,3,2,1,0:T(8,128)}) custom-call(f32[4,16,18,8,128]{4,3,2,1,0:T(8,128)} %get-tuple-element.54.refs_0_.refs_3_.refs_7_, f32[4,8,10,8,128]{4,3,2,1,0:T(8,128)} %get-tuple-element.75.refs_1_.refs_4_.refs_2_), custom_call_target="tpu_custom_call" | custom-call | tf_op jit(solution)/shard_map/pallas_call | solution.py:777
  59.1 8.7 %shard_map.51 = (f32[4,8,18,8,128]{4,3,2,1,0:T(8,128)}, bf16[2304,128]{1,0:T(8,128)(2,1)}, bf16[2304,128]{1,0:T(8,128)(2,1)}) custom-call(f32[4,16,18,8,128]{4,3,2,1,0:T(8,128)} %get-tuple-element.54.refs_0_.refs_3_.refs_7_, f32[4,8,22,8,128]{4,3,2,1,0:T(8,128)} %get-tuple-element.76.refs_1_, bf16[2304,128]{1,0:T(8,128)(2,1)} %copy-done, ...), custom_call_target="tpu_custom_call" | custom-call | tf_op jit(solution)/shard_map/pallas_call | solution.py:799
  67.8 3.9 %collective-permute-start.12 = (bf16[2304,128]{1,0:T(8,128)(2,1)}, bf16[2304,128]{1,0:T(8,128)(2,1)S(1)}, u32[]{:S(2)}, u32[]{:S(2)}) collective-permute-start(bf16[2304,128]{1,0:T(8,128)(2,1)} %get-tuple-element.84), channel_id=1, source_target_pairs={{0,1},{1,2},{2,3},{4,5},{5,6},{6,7},{8,9},{9,10},{10,11},{12,13},{... | collective-permute-start | bytes 1769480 | tf_op jit(solution)/shard_map/ppermute | solution.py:816
  71.8 1.3 %collective-permute-start.13 = (bf16[2304,128]{1,0:T(8,128)(2,1)}, bf16[2304,128]{1,0:T(8,128)(2,1)S(1)}, u32[]{:S(2)}, u32[]{:S(2)}) collective-permute-start(bf16[2304,128]{1,0:T(8,128)(2,1)} %get-tuple-element.85), channel_id=1, source_target_pairs={{1,0},{2,1},{3,2},{5,4},{6,5},{7,6},{9,8},{10,9},{11,10},{13,12},{... | collective-permute-start | bytes 1769480 | tf_op jit(solution)/shard_map/ppermute | solution.py:817
  73.1 10.8 %shard_map.52 = (f32[4,8,296,128]{3,2,1,0:T(8,128)}, f32[4,8,22,8,128]{4,3,2,1,0:T(8,128)}) custom-call(f32[4,8,18,8,128]{4,3,2,1,0:T(8,128)} %get-tuple-element.82.refs_0_, f32[4,8,18,8,128]{4,3,2,1,0:T(8,128)} %get-tuple-element.81.refs_1_.refs_0_, f32[4,8,10,8,128]{4,3,2,1,0:T(8,128)} %get-tuple-element.75.refs_1_.refs_4_.refs_2_, ...), custom_call_target="tpu_custom_call" | custom-call | tf_op jit(solution)/shard_map/pallas_call | solution.py:777
  83.9 3.5 %collective-permute-done.13.refs_3_ = bf16[2304,128]{1,0:T(8,128)(2,1)S(1)} collective-permute-done((bf16[2304,128]{1,0:T(8,128)(2,1)}, bf16[2304,128]{1,0:T(8,128)(2,1)S(1)}, u32[]{:S(2)}, u32[]{:S(2)}) %collective-permute-start.13) | collective-permute-done | bytes 589856 | tf_op jit(solution)/shard_map/ppermute | solution.py:817
  87.4 0.8 copy-done.5
  88.2 10.8 %shard_map.53 = f32[4,2048,128]{2,1,0:T(8,128)} custom-call(f32[4,8,18,8,128]{4,3,2,1,0:T(8,128)} %get-tuple-element.81.refs_1_.refs_0_, f32[4,8,22,8,128]{4,3,2,1,0:T(8,128)} %get-tuple-element.83.refs_1_, bf16[2304,128]{1,0:T(8,128)(2,1)} %copy-done.4, bf16[2304,128]{1,0:T(8,128)(2,1)} %copy-done.5, ...), custom_call_target="tpu_custom_call" | custom-call | tf_op jit(solution)/shard_map/pallas_call | solution.py:787
  (40 shorter events, 2.8 us)
Async XLA Ops:
  3.8 17.0 %collective-permute-start.2 = (bf16[1024,128]{1,0:T(8,128)(2,1)}, bf16[1024,128]{1,0:T(8,128)(2,1)S(1)}, u32[]{:S(2)}, u32[]{:S(2)}) collective-permute-start(bf16[1024,128]{1,0:T(8,128)(2,1)} %get-tuple-element.56), channel_id=1, source_target_pairs={{0,1},{1,2},{2,3},{3,0},{4,5},{5,6},{6,7},{7,4},{8,9},{9,10},{10,1... | collective-permute-start | bytes 786440 | tf_op jit(solution)/shard_map/ppermute | solution.py:826
  6.9 27.6 %collective-permute-start.3 = (bf16[1024,128]{1,0:T(8,128)(2,1)}, bf16[1024,128]{1,0:T(8,128)(2,1)S(1)}, u32[]{:S(2)}, u32[]{:S(2)}) collective-permute-start(bf16[1024,128]{1,0:T(8,128)(2,1)} %get-tuple-element.59), channel_id=1, source_target_pairs={{0,2},{1,3},{2,0},{3,1},{4,6},{5,7},{6,4},{7,5},{8,10},{9,11},{10,... | collective-permute-start | bytes 786440 | tf_op jit(solution)/shard_map/ppermute | solution.py:826
  9.5 25.1 %collective-permute-start.4 = (bf16[1024,128]{1,0:T(8,128)(2,1)}, bf16[1024,128]{1,0:T(8,128)(2,1)S(1)}, u32[]{:S(2)}, u32[]{:S(2)}) collective-permute-start(bf16[1024,128]{1,0:T(8,128)(2,1)} %get-tuple-element.60), channel_id=1, source_target_pairs={{0,3},{1,0},{2,1},{3,2},{4,7},{5,4},{6,5},{7,6},{8,11},{9,8},{10,9... | collective-permute-start | bytes 786440 | tf_op jit(solution)/shard_map/ppermute | solution.py:826
  10.9 2.6 %collective-permute-start = (bf16[768,128]{1,0:T(8,128)(2,1)}, bf16[768,128]{1,0:T(8,128)(2,1)S(1)}, u32[]{:S(2)}, u32[]{:S(2)}) collective-permute-start(bf16[768,128]{1,0:T(8,128)(2,1)} %get-tuple-element.46), channel_id=1, source_target_pairs={{0,4},{4,8},{8,12},{12,16},{16,20},{20,24},{24,28},{1,5},{5,9},{9,... | collective-permute-start | bytes 589832 | tf_op jit(solution)/shard_map/ppermute | solution.py:816
  12.2 5.3 %collective-permute-start.1 = (bf16[768,128]{1,0:T(8,128)(2,1)}, bf16[768,128]{1,0:T(8,128)(2,1)S(1)}, u32[]{:S(2)}, u32[]{:S(2)}) collective-permute-start(bf16[768,128]{1,0:T(8,128)(2,1)} %get-tuple-element.47), channel_id=1, source_target_pairs={{4,0},{8,4},{12,8},{16,12},{20,16},{24,20},{28,24},{5,1},{9,5},{13... | collective-permute-start | bytes 589832 | tf_op jit(solution)/shard_map/ppermute | solution.py:817
  13.5 4.0 %copy-start.2 = (bf16[768,128]{1,0:T(8,128)(2,1)}, bf16[768,128]{1,0:T(8,128)(2,1)S(1)}, u32[]{:S(2)}) copy-start(bf16[768,128]{1,0:T(8,128)(2,1)S(1)} %collective-permute-done.before) | copy-start | bytes 589828
  19.8 9.9 %collective-permute-start.5 = (bf16[128,128]{1,0:T(8,128)(2,1)}, bf16[128,128]{1,0:T(8,128)(2,1)S(1)}, u32[]{:S(2)}, u32[]{:S(2)}) collective-permute-start(bf16[128,128]{1,0:T(8,128)(2,1)} %get-tuple-element.62), channel_id=1, source_target_pairs={{0,1},{1,2},{2,3},{3,0},{4,5},{5,6},{6,7},{7,4},{8,9},{9,10},{10,1... | collective-permute-start | bytes 98312 | tf_op jit(solution)/shard_map/ppermute | solution.py:826
  20.5 14.1 %collective-permute-start.6 = (bf16[128,128]{1,0:T(8,128)(2,1)}, bf16[128,128]{1,0:T(8,128)(2,1)S(1)}, u32[]{:S(2)}, u32[]{:S(2)}) collective-permute-start(bf16[128,128]{1,0:T(8,128)(2,1)} %get-tuple-element.63), channel_id=1, source_target_pairs={{0,2},{1,3},{2,0},{3,1},{4,6},{5,7},{6,4},{7,5},{8,10},{9,11},{10,... | collective-permute-start | bytes 98312 | tf_op jit(solution)/shard_map/ppermute | solution.py:826
  20.8 18.1 %copy-start.8 = (bf16[1024,128]{1,0:T(8,128)(2,1)}, bf16[1024,128]{1,0:T(8,128)(2,1)S(1)}, u32[]{:S(2)}) copy-start(bf16[1024,128]{1,0:T(8,128)(2,1)S(1)} %collective-permute-done.2.refs_1_) | copy-start | bytes 786436
  20.8 13.7 %collective-permute-start.7 = (bf16[128,128]{1,0:T(8,128)(2,1)}, bf16[128,128]{1,0:T(8,128)(2,1)S(1)}, u32[]{:S(2)}, u32[]{:S(2)}) collective-permute-start(bf16[128,128]{1,0:T(8,128)(2,1)} %get-tuple-element.64), channel_id=1, source_target_pairs={{0,3},{1,0},{2,1},{3,2},{4,7},{5,4},{6,5},{7,6},{8,11},{9,8},{10,9... | collective-permute-start | bytes 98312 | tf_op jit(solution)/shard_map/ppermute | solution.py:826
  29.8 9.2 %copy-start.11 = (bf16[128,128]{1,0:T(8,128)(2,1)}, bf16[128,128]{1,0:T(8,128)(2,1)S(1)}, u32[]{:S(2)}) copy-start(bf16[128,128]{1,0:T(8,128)(2,1)S(1)} %collective-permute-done.5.refs_5_) | copy-start | bytes 98308
  34.6 4.4 %copy-start.12 = (bf16[128,128]{1,0:T(8,128)(2,1)}, bf16[128,128]{1,0:T(8,128)(2,1)S(1)}, u32[]{:S(2)}) copy-start(bf16[128,128]{1,0:T(8,128)(2,1)S(1)} %collective-permute-done.6.refs_6_) | copy-start | bytes 98308
  34.6 4.4 %copy-start.9 = (bf16[1024,128]{1,0:T(8,128)(2,1)}, bf16[1024,128]{1,0:T(8,128)(2,1)S(1)}, u32[]{:S(2)}) copy-start(bf16[1024,128]{1,0:T(8,128)(2,1)S(1)} %collective-permute-done.3.refs_2_) | copy-start | bytes 786436
  34.6 4.4 %copy-start.10 = (bf16[1024,128]{1,0:T(8,128)(2,1)}, bf16[1024,128]{1,0:T(8,128)(2,1)S(1)}, u32[]{:S(2)}) copy-start(bf16[1024,128]{1,0:T(8,128)(2,1)S(1)} %collective-permute-done.4.refs_3_) | copy-start | bytes 786436
  34.6 4.4 %copy-start.13 = (bf16[128,128]{1,0:T(8,128)(2,1)}, bf16[128,128]{1,0:T(8,128)(2,1)S(1)}, u32[]{:S(2)}) copy-start(bf16[128,128]{1,0:T(8,128)(2,1)S(1)} %collective-permute-done.7.refs_7_) | copy-start | bytes 98308
  34.6 23.4 %collective-permute-start.8 = (bf16[2304,128]{1,0:T(8,128)(2,1)}, bf16[2304,128]{1,0:T(8,128)(2,1)S(1)}, u32[]{:S(2)}, u32[]{:S(2)}) collective-permute-start(bf16[2304,128]{1,0:T(8,128)(2,1)} %get-tuple-element.77), channel_id=1, source_target_pairs={{0,1},{1,2},{2,3},{4,5},{5,6},{6,7},{8,9},{9,10},{10,11},{12,13},{... | collective-permute-start | bytes 1769480 | tf_op jit(solution)/shard_map/ppermute | solution.py:816
  37.7 20.4 %collective-permute-start.9 = (bf16[2304,128]{1,0:T(8,128)(2,1)}, bf16[2304,128]{1,0:T(8,128)(2,1)S(1)}, u32[]{:S(2)}, u32[]{:S(2)}) collective-permute-start(bf16[2304,128]{1,0:T(8,128)(2,1)} %get-tuple-element.78), channel_id=1, source_target_pairs={{1,0},{2,1},{3,2},{5,4},{6,5},{7,6},{9,8},{10,9},{11,10},{13,12},{... | collective-permute-start | bytes 1769480 | tf_op jit(solution)/shard_map/ppermute | solution.py:817
  42.6 15.4 %collective-permute-start.11 = (bf16[576,128]{1,0:T(8,128)(2,1)}, bf16[576,128]{1,0:T(8,128)(2,1)S(1)}, u32[]{:S(2)}, u32[]{:S(2)}) collective-permute-start(bf16[576,128]{1,0:T(8,128)(2,1)} %get-tuple-element.80), channel_id=1, source_target_pairs={{1,0},{2,1},{3,2},{5,4},{6,5},{7,6},{9,8},{10,9},{11,10},{13,12},{... | collective-permute-start | bytes 442376 | tf_op jit(solution)/shard_map/ppermute | solution.py:817
  43.9 14.1 %collective-permute-start.10 = (bf16[288,128]{1,0:T(8,128)(2,1)}, bf16[288,128]{1,0:T(8,128)(2,1)S(1)}, u32[]{:S(2)}, u32[]{:S(2)}) collective-permute-start(bf16[288,128]{1,0:T(8,128)(2,1)} %get-tuple-element.79), channel_id=1, source_target_pairs={{0,1},{1,2},{2,3},{4,5},{5,6},{6,7},{8,9},{9,10},{10,11},{12,13},{... | collective-permute-start | bytes 221192 | tf_op jit(solution)/shard_map/ppermute | solution.py:816
  58.0 0.9 copy-start
  58.1 1.0 %copy-start.1 = (bf16[2304,128]{1,0:T(8,128)(2,1)}, bf16[2304,128]{1,0:T(8,128)(2,1)S(1)}, u32[]{:S(2)}) copy-start(bf16[2304,128]{1,0:T(8,128)(2,1)S(1)} %collective-permute-done.9.refs_3_.refs_9_) | copy-start | bytes 1769476
  67.8 16.1 %collective-permute-start.12 = (bf16[2304,128]{1,0:T(8,128)(2,1)}, bf16[2304,128]{1,0:T(8,128)(2,1)S(1)}, u32[]{:S(2)}, u32[]{:S(2)}) collective-permute-start(bf16[2304,128]{1,0:T(8,128)(2,1)} %get-tuple-element.84), channel_id=1, source_target_pairs={{0,1},{1,2},{2,3},{4,5},{5,6},{6,7},{8,9},{9,10},{10,11},{12,13},{... | collective-permute-start | bytes 1769480 | tf_op jit(solution)/shard_map/ppermute | solution.py:816
  71.8 15.7 %collective-permute-start.13 = (bf16[2304,128]{1,0:T(8,128)(2,1)}, bf16[2304,128]{1,0:T(8,128)(2,1)S(1)}, u32[]{:S(2)}, u32[]{:S(2)}) collective-permute-start(bf16[2304,128]{1,0:T(8,128)(2,1)} %get-tuple-element.85), channel_id=1, source_target_pairs={{1,0},{2,1},{3,2},{5,4},{6,5},{7,6},{9,8},{10,9},{11,10},{13,12},{... | collective-permute-start | bytes 1769480 | tf_op jit(solution)/shard_map/ppermute | solution.py:817
  83.9 3.5 %copy-start.4 = (bf16[2304,128]{1,0:T(8,128)(2,1)}, bf16[2304,128]{1,0:T(8,128)(2,1)S(1)}, u32[]{:S(2)}) copy-start(bf16[2304,128]{1,0:T(8,128)(2,1)S(1)} %collective-permute-done.12.refs_2_) | copy-start | bytes 1769476
  (4 other events, 2.8 us)
